TPU v7x, 256 devices: a whole 4x4x8 slice. The times are simulated.
256 devices in a mesh: seq: 128 (over x, z_lo, y, core), dp: 2 (over z_hi).
Axes of the slice: x: 4, y: 4, z: 8 (z_hi: 2, z_lo: 4; z = z_hi * 4 + z_lo), core: 2. Of those that a mesh axis runs over, the one named last changes fastest.
Arguments:
- queries: bfloat16 [2, 32768, 1024], P('dp', 'seq'), may hold values from -8 to 8
- keys: bfloat16 [2, 32768, 1024], P('dp', 'seq'), may hold values from -8 to 8
- values: bfloat16 [2, 32768, 1024], P('dp', 'seq'), may hold values from -6 to 6
- out_grad: bfloat16 [2, 32768, 1024], P('dp', 'seq'), may hold values from -6 to 6
- out_weight: bfloat16 [1024, 1024], replicated, may hold values from -0.1875 to 0.1875
Outputs:
- q_grad: bfloat16 [2, 32768, 1024], P('dp', 'seq')
- k_grad: bfloat16 [2, 32768, 1024], P('dp', 'seq')
- v_grad: bfloat16 [2, 32768, 1024], P('dp', 'seq')
- wo_grad: float32 [1024, 1024], P('seq', 'dp')
All inputs are finite; a program needn't handle non-finite values.
Results may differ from a plain program's by a relative error of at most 0.017.
Values may be sent and summed in bfloat16 or wider, within the bound.
A program may use at most 64 MiB of HBM per device.

v0:
```python
import math

import jax
import jax.numpy as jnp
from jax import lax
from jax.sharding import PartitionSpec as P

HEAD_DIM = 64
HALF = 128


masked_score = -1e30


def extended(cells, sides, width):
    for axis, dim in sides:
        count = lax.axis_size(axis)
        ends = count - 1
        head = lax.slice_in_dim(cells, 0, width, axis=dim)
        tail = lax.slice_in_dim(cells, cells.shape[dim] - width, cells.shape[dim], axis=dim)
        cells = jnp.concatenate(
            [
                lax.ppermute(tail, axis, [(i, (i + 1) % count) for i in range(ends)]),
                cells,
                lax.ppermute(head, axis, [((i + 1) % count, i) for i in range(ends)]),
            ],
            axis=dim,
        )
    return cells


def passed_along(value, axis, steps):
    count = lax.axis_size(axis)
    first, last = (max(0, -steps), min(count, count - steps))
    return lax.ppermute(value, axis, [(source, source + steps) for source in range(first, last)])


def attend(query_rows, key_rows, value_rows, dattn_rows, query_first, key_first, seq_total):
    count_q, model_width = query_rows.shape
    count_k = key_rows.shape[0]
    head_count = model_width // HEAD_DIM
    group_size = math.gcd(4, head_count)
    scaling = HEAD_DIM ** (-0.5)
    query_pos = query_first + jnp.arange(count_q, dtype=jnp.int32)
    key_pos = key_first + jnp.arange(count_k, dtype=jnp.int32)
    inside = (key_pos[None, :] >= query_pos[:, None] - HALF) & (
        key_pos[None, :] < query_pos[:, None] + HALF
    )
    inside = inside & (key_pos[None, :] >= 0) & (key_pos[None, :] < seq_total)
    inside = inside & (query_pos[:, None] >= 0) & (query_pos[:, None] < seq_total)
    attended_list = []
    total_list = []
    delta_list = []
    query_grads = []
    key_grads = []
    value_grads = []
    for group_index in range(head_count // group_size):
        head_start = group_index * group_size
        col_start = head_start * HEAD_DIM
        col_end = col_start + group_size * HEAD_DIM
        query_head = query_rows[:, col_start:col_end].reshape(count_q, group_size, HEAD_DIM)
        key_head = key_rows[:, col_start:col_end].reshape(count_k, group_size, HEAD_DIM)
        value_head = value_rows[:, col_start:col_end].reshape(count_k, group_size, HEAD_DIM)
        dattn_head = dattn_rows[:, col_start:col_end].reshape(count_q, group_size, HEAD_DIM)
        scores = (
            jnp.einsum("qhd,khd->hqk", query_head, key_head, preferred_element_type=jnp.float32)
            * scaling
        )
        scores = jnp.where(inside[None], scores, masked_score)
        row_max = jnp.max(scores, axis=-1, keepdims=True)
        log_total = row_max + jnp.log(jnp.sum(jnp.exp(scores - row_max), axis=-1, keepdims=True))
        weights = jnp.exp(scores - log_total)
        weights_bf = weights.astype(jnp.bfloat16)
        attended = jnp.einsum(
            "hqk,khd->qhd", weights_bf, value_head, preferred_element_type=jnp.float32
        ).astype(jnp.bfloat16)
        row_delta = jnp.sum(dattn_head.astype(jnp.float32) * attended.astype(jnp.float32), axis=-1)
        attended_list.append(attended.reshape(count_q, group_size * HEAD_DIM))
        total_list.append(log_total[:, :, 0].T)
        delta_list.append(row_delta)
        value_grads.append(
            jnp.einsum(
                "hqk,qhd->khd", weights_bf, dattn_head, preferred_element_type=jnp.float32
            ).reshape(count_k, -1)
        )
        dweights = jnp.einsum(
            "qhd,khd->hqk", dattn_head, value_head, preferred_element_type=jnp.float32
        )
        dscore = (weights * (dweights - row_delta.T[:, :, None])).astype(jnp.bfloat16)
        query_grads.append(
            (
                jnp.einsum("hqk,khd->qhd", dscore, key_head, preferred_element_type=jnp.float32)
                * scaling
            ).reshape(count_q, -1)
        )
        key_grads.append(
            (
                jnp.einsum("hqk,qhd->khd", dscore, query_head, preferred_element_type=jnp.float32)
                * scaling
            ).reshape(count_k, -1)
        )
    attended_all = None
    statistics = None
    query_grad = None
    pair_grad = None
    attended_all = jnp.concatenate(attended_list, axis=1)
    statistics = jnp.stack(
        [jnp.concatenate(total_list, axis=1), jnp.concatenate(delta_list, axis=1)]
    )
    query_grad = jnp.concatenate(query_grads, axis=1)
    pair_grad = jnp.concatenate(key_grads + value_grads, axis=1)
    return (attended_all, statistics, query_grad, pair_grad)


def tiled(query_rows, key_rows, value_rows, dattn_rows, query_first, lead, seq_total):
    count_q, model_width = query_rows.shape
    count_k = key_rows.shape[0]
    key_padded = jnp.pad(key_rows, ((HALF, HALF), (0, 0)))
    value_padded = jnp.pad(value_rows, ((HALF, HALF), (0, 0)))
    span = 3 * HALF
    attended_list = []
    stats_list = []
    query_list = []
    pair_total = None
    pair_total = jnp.zeros((count_k + 2 * HALF, 2 * model_width), jnp.float32)
    for block_index in range(count_q // HALF):
        row_lo = block_index * HALF
        key_lo = lead + row_lo
        block_first = query_first + row_lo
        attended, statistics, query_grad, pair_grad = attend(
            query_rows[row_lo : row_lo + HALF],
            key_padded[key_lo : key_lo + span],
            value_padded[key_lo : key_lo + span],
            dattn_rows[row_lo : row_lo + HALF],
            block_first,
            block_first - HALF,
            seq_total,
        )
        attended_list.append(attended)
        stats_list.append(statistics)
        query_list.append(query_grad)
        pair_total = pair_total.at[key_lo : key_lo + span].add(pair_grad)
    attended_all = None
    stats_all = None
    query_all = None
    pair_all = None
    attended_all = jnp.concatenate(attended_list, axis=0)
    stats_all = jnp.concatenate(stats_list, axis=1)
    query_all = jnp.concatenate(query_list, axis=0)
    pair_all = pair_total[HALF : HALF + count_k]
    return (attended_all, stats_all, query_all, pair_all)


def on_device(queries, keys, values, out_grad, out_weight):
    query_rows = queries[0]
    key_rows = keys[0]
    value_rows = values[0]
    grad_rows = out_grad[0]
    row_count, model_width = query_rows.shape
    seq_devices = lax.axis_size("seq")
    seq_total = row_count * seq_devices
    first_row = lax.axis_index("seq") * row_count
    dattn = lax.dot_general(
        grad_rows, out_weight, (((1,), (1,)), ((), ())), preferred_element_type=jnp.float32
    ).astype(jnp.bfloat16)
    paired = jnp.concatenate([key_rows, value_rows], axis=1)
    widened = extended(paired, (("seq", 0),), HALF)
    key_wide = widened[:, :model_width]
    value_wide = widened[:, model_width:]
    attended, statistics, query_grad, pair_grad = tiled(
        query_rows, key_wide, value_wide, dattn, first_row, HALF, seq_total
    )
    lower_rim = pair_grad[:HALF]
    upper_rim = pair_grad[row_count + HALF :]
    from_above = passed_along(lower_rim.astype(jnp.bfloat16), "seq", -1).astype(lower_rim.dtype)
    from_below = passed_along(upper_rim, "seq", 1)
    middle = pair_grad[HALF : HALF + row_count]
    padding = row_count - HALF
    pair_local = (
        middle
        + jnp.pad(from_below, ((0, padding), (0, 0)))
        + jnp.pad(from_above, ((padding, 0), (0, 0)))
    )
    key_grad = pair_local[:, :model_width].astype(jnp.bfloat16)
    value_grad = pair_local[:, model_width:].astype(jnp.bfloat16)
    frames = row_count * seq_devices * lax.axis_size("dp")
    summed = lax.psum_scatter(
        lax.dot_general(
            attended, grad_rows, (((0,), (0,)), ((), ())), preferred_element_type=jnp.float32
        ),
        "seq",
        scatter_dimension=0,
        tiled=True,
    )
    summed = lax.psum_scatter(summed, "dp", scatter_dimension=1, tiled=True)
    wo_grad = summed * frames ** (-0.5)
    return (query_grad.astype(jnp.bfloat16)[None], key_grad[None], value_grad[None], wo_grad)


def solution(mesh):
    in_specs = (
        P("dp", "seq", None),
        P("dp", "seq", None),
        P("dp", "seq", None),
        P("dp", "seq", None),
        P(),
    )
    out_specs = (P("dp", "seq", None), P("dp", "seq", None), P("dp", "seq", None), P("seq", "dp"))
    return jax.shard_map(
        on_device, mesh=mesh, in_specs=in_specs, out_specs=out_specs, check_vma=False
    )
```

profile of v0, /device:TPU:96, one launch (start us, length us, event | category | flops | bytes accessed | tf_op | source)
XLA Modules:
  0.0 807.4 jit_solution(12395104438888884436)
XLA Ops:
  7.2 2.4 fusion.51
  9.6 1.9 collective-permute-start
  11.5 5.8 collective-permute-start.1
  18.4 1.8 convolution_convert_fusion
  22.9 1.6 copy.155
  24.4 1.6 copy.144
  29.3 1.6 copy.122
  35.7 1.6 copy.168
  40.7 1.6 maximum_maximum_fusion
  67.9 1.8 copy.131
  71.3 1.8 copy.156
  73.1 2.0 copy.212
  75.1 1.6 copy.184
  76.7 1.9 copy.216
  78.6 2.0 copy.211
  82.1 2.0 copy.215
  84.1 1.9 copy.210
  87.6 1.9 copy.214
  98.5 2.7 fusion.52
  101.3 1.6 fusion.31
  102.9 1.9 convolution_multiply_fusion.11
  104.8 1.9 copy.209
  106.7 1.8 fusion.39
  113.9 1.9 convolution_multiply_fusion.15
  115.8 1.9 copy.193
  117.7 1.8 fusion.35
  119.5 1.6 copy.149
  123.4 1.6 fusion.28
  125.0 1.9 convolution_multiply_fusion.14
  126.9 1.9 copy.194
  128.9 2.2 fusion.88
  131.1 2.0 copy.198
  133.0 1.6 fusion.29
  135.4 1.9 convolution_multiply_fusion.13
  137.3 1.9 copy.195
  139.2 2.2 fusion.85
  141.4 1.9 copy.199
  145.3 1.9 convolution_multiply_fusion.12
  147.2 1.9 copy.196
  150.2 2.0 copy.200
  159.0 1.7 copy-done.5
  161.8 1.9 collective-permute-start.2
  165.3 5.8 collective-permute-start.3
  174.1 4.3 collective-permute-done.3
  178.4 2.4 collective-permute-done.2
  180.9 2.3 fusion.2
  183.2 518.4 %reduce-scatter.3.cloned.1.call-done = f32[8,1024]{1,0:T(8,128)} async-done(((f32[1024,1024]{1,0:T(8,128)}), f32[8,1024]{1,0:T(8,128)}) %reduce-scatter.3.cloned.1.call-update) | async-done | bytes 32784 | tf_op jit(solution)/shard_map/reduce_scatter | solution.py:187
  702.6 96.6 %reduce-scatter.5.cloned.1.call-done = f32[8,512]{1,0:T(8,128)} async-done(((f32[8,1024]{1,0:T(8,128)}), f32[8,512]{1,0:T(8,128)}) %reduce-scatter.5.cloned.1.call-update) | async-done | bytes 16400 | tf_op jit(solution)/shard_map/reduce_scatter | solution.py:195
  (247 shorter events, 80.2 us)
Async XLA Ops:
  7.2 11.3 %copy-start = (bf16[1024,1024]{1,0:T(8,128)(2,1)S(1)}, bf16[1024,1024]{1,0:T(8,128)(2,1)}, u32[]{:S(2)}) copy-start(bf16[1024,1024]{1,0:T(8,128)(2,1)} %param.13) | copy-start | bytes 6291460
  7.2 694.4 %reduce-scatter.3.cloned.1.call-start = ((), (), s32[]{:S(2)}) async-start(), calls=%async_computation.2 | async-start | bytes 4227072 | tf_op jit(solution)/shard_map/reduce_scatter | solution.py:187
  9.6 31.1 %collective-permute-start = (bf16[128,2048]{1,0:T(8,128)(2,1)}, bf16[128,2048]{1,0:T(8,128)(2,1)}, u32[]{:S(2)}, u32[]{:S(2)}) collective-permute-start(bf16[128,2048]{1,0:T(8,128)(2,1)} %get-tuple-element.48), channel_id=1, source_target_pairs={{0,2},{2,4},{4,6},{6,8},{8,10},{10,12},{12,14},{14,16},{16,18},{18... | collective-permute-start | bytes 1572872 | tf_op jit(solution)/shard_map/ppermute | solution.py:23
  11.5 29.2 %collective-permute-start.1 = (bf16[128,2048]{1,0:T(8,128)(2,1)}, bf16[128,2048]{1,0:T(8,128)(2,1)}, u32[]{:S(2)}, u32[]{:S(2)}) collective-permute-start(bf16[128,2048]{1,0:T(8,128)(2,1)} %get-tuple-element.49), channel_id=1, source_target_pairs={{2,0},{4,2},{6,4},{8,6},{10,8},{12,10},{14,12},{16,14},{18,16},{20... | collective-permute-start | bytes 1572872 | tf_op jit(solution)/shard_map/ppermute | solution.py:25
  20.2 20.5 %copy-start.10 = (bf16[1,256,1024]{2,1,0:T(8,128)(2,1)S(1)}, bf16[1,256,1024]{2,1,0:T(8,128)(2,1)}, u32[]{:S(2)}) copy-start(bf16[1,256,1024]{2,1,0:T(8,128)(2,1)} %param.11) | copy-start | bytes 1572868
  20.2 20.5 %copy-start.11 = (bf16[1,256,1024]{2,1,0:T(8,128)(2,1)S(1)}, bf16[1,256,1024]{2,1,0:T(8,128)(2,1)}, u32[]{:S(2)}) copy-start(bf16[1,256,1024]{2,1,0:T(8,128)(2,1)} %param.10) | copy-start | bytes 1572868
  35.7 23.1 %copy-start.47 = (bf16[128,256]{0,1:T(8,128)(2,1)}, bf16[128,256]{0,1:T(8,128)(2,1)S(1)}, u32[]{:S(2)}) copy-start(bf16[128,256]{0,1:T(8,128)(2,1)S(1)} %copy.161) | copy-start | bytes 196612
  40.7 18.1 %copy-start.34 = (pred[128,384]{0,1:T(8,128)(4,1)}, pred[128,384]{0,1:T(8,128)(4,1)S(1)}, u32[]{:S(2)}) copy-start(pred[128,384]{0,1:T(8,128)(4,1)S(1)} %and_and_fusion) | copy-start | bytes 147460
  45.0 3.7 copy-start.51
  45.5 6.4 copy-start.49
  59.1 3.3 copy-start.48
  59.2 5.2 copy-start.43
  64.5 33.2 %copy-start.17 = (bf16[384,256]{0,1:T(8,128)(2,1)}, bf16[384,256]{0,1:T(8,128)(2,1)S(1)}, u32[]{:S(2)}) copy-start(bf16[384,256]{0,1:T(8,128)(2,1)S(1)} %copy.145) | copy-start | bytes 589828
  66.8 30.1 %copy-start.18 = (bf16[384,256]{0,1:T(8,128)(2,1)}, bf16[384,256]{0,1:T(8,128)(2,1)S(1)}, u32[]{:S(2)}) copy-start(bf16[384,256]{0,1:T(8,128)(2,1)S(1)} %copy.138) | copy-start | bytes 589828
  67.9 25.0 %copy-start.12 = (bf16[384,256]{0,1:T(8,128)(2,1)}, bf16[384,256]{0,1:T(8,128)(2,1)S(1)}, u32[]{:S(2)}) copy-start(bf16[384,256]{0,1:T(8,128)(2,1)S(1)} %copy.135) | copy-start | bytes 589828
  69.9 22.4 %copy-start.13 = (bf16[384,256]{0,1:T(8,128)(2,1)}, bf16[384,256]{0,1:T(8,128)(2,1)S(1)}, u32[]{:S(2)}) copy-start(bf16[384,256]{0,1:T(8,128)(2,1)S(1)} %copy.128) | copy-start | bytes 589828
  70.1 20.8 %copy-start.15 = (bf16[384,256]{0,1:T(8,128)(2,1)}, bf16[384,256]{0,1:T(8,128)(2,1)S(1)}, u32[]{:S(2)}) copy-start(bf16[384,256]{0,1:T(8,128)(2,1)S(1)} %copy.121) | copy-start | bytes 589828
  71.3 19.5 %copy-start.16 = (bf16[384,256]{0,1:T(8,128)(2,1)}, bf16[384,256]{0,1:T(8,128)(2,1)S(1)}, u32[]{:S(2)}) copy-start(bf16[384,256]{0,1:T(8,128)(2,1)S(1)} %copy.153) | copy-start | bytes 589828
  89.5 3.4 copy-start.45
  90.7 3.2 copy-start.4
  90.9 3.1 copy-start.56
  92.7 3.2 copy-start.2
  92.9 3.1 copy-start.19
  92.9 3.0 copy-start.40
  93.3 4.4 copy-start.1
  93.3 3.5 copy-start.37
  93.4 4.3 copy-start.35
  93.8 4.7 copy-start.52
  93.8 4.7 copy-start.53
  93.8 4.7 copy-start.54
  93.8 4.7 copy-start.55
  101.2 11.2 %copy-start.39 = (bf16[128,256]{0,1:T(8,128)(2,1)S(1)}, bf16[128,256]{0,1:T(8,128)(2,1)}, u32[]{:S(2)}) copy-start(bf16[128,256]{0,1:T(8,128)(2,1)} %copy.123) | copy-start | bytes 196612
  101.2 698.0 %reduce-scatter.5.cloned.1.call-start = ((), (), s32[]{:S(2)}) async-start(), calls=%async_computation.3 | async-start | bytes 49152 | tf_op jit(solution)/shard_map/reduce_scatter | solution.py:195
  122.5 6.4 copy-start.41
  122.5 10.5 %copy-start.58 = (f32[128,4]{0,1:T(4,128)S(1)}, f32[128,4]{0,1:T(4,128)}, u32[]{:S(2)}) copy-start(f32[128,4]{0,1:T(4,128)} %get-tuple-element.90) | copy-start | bytes 6148
  131.1 12.3 %copy-start.36 = (bf16[128,256]{0,1:T(8,128)(2,1)S(1)}, bf16[128,256]{0,1:T(8,128)(2,1)}, u32[]{:S(2)}) copy-start(bf16[128,256]{0,1:T(8,128)(2,1)} %copy.144) | copy-start | bytes 196612
  131.1 12.3 %copy-start.57 = (f32[128,4]{0,1:T(4,128)S(1)}, f32[128,4]{0,1:T(4,128)}, u32[]{:S(2)}) copy-start(f32[128,4]{0,1:T(4,128)} %get-tuple-element.86) | copy-start | bytes 6148
  150.2 6.4 copy-start.30
  150.2 6.5 copy-start.31
  152.2 4.6 copy-start.32
  152.2 4.7 copy-start.33
  153.3 4.5 copy-start.28
  154.4 3.4 copy-start.27
  158.4 5.3 copy-start.14
  158.4 5.6 copy-start.7
  160.6 10.4 %copy-start.9 = (bf16[4,128,384]{1,2,0:T(8,128)(2,1)S(1)}, bf16[4,128,384]{1,2,0:T(8,128)(2,1)}, u32[]{:S(2)}) copy-start(bf16[4,128,384]{1,2,0:T(8,128)(2,1)} %copy-done.8) | copy-start | bytes 1179652
  161.8 19.1 %collective-permute-start.2 = (f32[128,2048]{1,0:T(8,128)}, f32[128,2048]{1,0:T(8,128)}, u32[]{:S(2)}, u32[]{:S(2)}) collective-permute-start(f32[128,2048]{1,0:T(8,128)} %slice.309), channel_id=1, source_target_pairs={{0,2},{2,4},{4,6},{6,8},{8,10},{10,12},{12,14},{14,16},{16,18},{18... | collective-permute-start | bytes 3145736 | tf_op jit(solution)/shard_map/ppermute | solution.py:35
  165.3 13.1 %collective-permute-start.3 = (bf16[128,2048]{1,0:T(8,128)(2,1)}, bf16[128,2048]{1,0:T(8,128)(2,1)}, u32[]{:S(2)}, u32[]{:S(2)}) collective-permute-start(bf16[128,2048]{1,0:T(8,128)(2,1)} %slice.332), channel_id=1, source_target_pairs={{2,0},{4,2},{6,4},{8,6},{10,8},{12,10},{14,12},{16,14},{18,16},{20... | collective-permute-start | bytes 1572872 | tf_op jit(solution)/shard_map/ppermute | solution.py:35
  (17 other events, 32.2 us)
Sparse Core Ops, SparseCore 0:
  101.3 600.1 reduce-scatter.2
  704.1 95.0 reduce-scatter.4
where the time goes:
time: 814 us; the launch traced here: 807 us
  waiting for transfers between devices  622 us (76%)
  local copies, waits for them, and re-layouts  84.5 us (10%)
  matrix products  56.4 us (7%)
  starting transfers between devices  15.4 us (2%)
  between operations  15.2 us (2%)
  other arithmetic  14 us (2%)
    reduce_scatter x1, waiting for transfers between devices, on_device(): lax.psum_scatter(lax.dot_general(attended, grad_rows, (((0,), (0,)), ((),...  518 us
    reduce_scatter x1, waiting for transfers between devices, on_device(): summed = lax.psum_scatter(summed, 'dp', scatter_dimension=1, tiled=True)  96.6 us
  transfers between devices with their start and end apart: 6, of which 4 were waited for; matrix products, arithmetic and copies ran while one was open for 11% of the time, Pallas kernels for 0%

commit v1 on v0

v1 whole, which is shorter than its diff:
```python
import functools

import jax
import jax.numpy as jnp
from jax import lax
from jax.experimental import pallas as pl
from jax.experimental.pallas import tpu as pltpu
from jax.sharding import PartitionSpec as P

HEAD = 64
HALF = 128
BF = jnp.bfloat16
F32 = jnp.float32
NEG = -1e30
NX, NZ, NY, NC = 4, 4, 4, 2
GROUPS = 4
GW = 256
NT = (((1,), (1,)), ((), ()))
NN = (((1,), (0,)), ((), ()))
SCALE = HEAD ** -0.5


def dot(a, b, dims=NN):
    return lax.dot_general(a, b, dims, preferred_element_type=F32)


def kernel(n_seq, n_dp, q_h, k_h, v_h, g_h, w_h, qo, ko, vo, wo,
           q_s, k_s, v_s, og, w_s, k_t, v_t, q_st, d_st, p_s, a_t, bias,
           part, cs, cr, xs, xr, ysend, yrecv, zs, zr, rs, rr, own,
           load_sem, hsend, hrecv, csend, crecv, xsend, xrecv, ysem, yrsem,
           zsem, zrsem, rsend, rrecv):
    me = lax.axis_index("seq")
    zh = lax.axis_index("dp")
    c = me % NC
    y = (me // NC) % NY
    zl = (me // (NC * NY)) % NZ
    x = me // (NC * NY * NZ)
    rows = 2 * HALF

    def at(x_, z_, y_, c_):
        return ((x_ * NZ + z_) * NY + y_) * NC + c_

    prev = (me + n_seq - 1) % n_seq
    nxt = (me + 1) % n_seq
    mate = at(x, zl, y, 1 - c)
    x_up = at((x + 1) % NX, zl, y, c)
    x_dn = at((x + NX - 1) % NX, zl, y, c)
    x_far = at((x + 1 + (NX - 2) * c) % NX, zl, y, c)
    y_to = [at(x, zl, (y + i) % NY, c) for i in range(1, NY)]
    z_me = zh * NZ + zl
    z_all = [(z_me + i) % (NZ * n_dp) for i in range(1, NZ * n_dp)]
    z_to = [(at(x, z % NZ, y, c), z // NZ) for z in z_all]

    def remote(src, dst, ss, rsem, seq, dp=None):
        return pltpu.make_async_remote_copy(
            src_ref=src, dst_ref=dst, send_sem=ss, recv_sem=rsem,
            device_id={"seq": seq, "dp": zh if dp is None else dp},
            device_id_type=pl.DeviceIdType.MESH)

    barrier = pltpu.get_barrier_semaphore()
    partners = [(prev, zh), (nxt, zh), (x_up, zh), (x_dn, zh)]
    partners += [(s, zh) for s in y_to] + z_to
    for s, d in partners:
        pl.semaphore_signal(barrier, inc=1, device_id={"seq": s, "dp": d},
                            device_id_type=pl.DeviceIdType.MESH)

    loads = [pltpu.make_async_copy(g_h, og, load_sem.at[0]),
             pltpu.make_async_copy(w_h, w_s, load_sem.at[1])]
    for g in range(GROUPS):
        cols = pl.ds(g * GW, GW)
        loads.append(pltpu.make_async_copy(q_h.at[:, cols], q_s.at[g], load_sem.at[2 + g]))
        loads.append(pltpu.make_async_copy(
            k_h.at[:, cols], k_s.at[g, pl.ds(HALF, rows)], load_sem.at[6 + g]))
        loads.append(pltpu.make_async_copy(
            v_h.at[:, cols], v_s.at[g, pl.ds(HALF, rows)], load_sem.at[10 + g]))
    for cp in loads:
        cp.start()

    pl.semaphore_wait(barrier, len(partners))

    order = [(x + 2) % NX, (x + 1) % NX, (x + 3) % NX, x]
    halos = []
    for g in order:
        cols = pl.ds(pl.multiple_of(g * GW, GW), GW)
        mine = []
        for a, (src, dst) in enumerate(((k_h, k_s), (v_h, v_s))):
            mine.append(remote(src.at[pl.ds(HALF, HALF), cols], dst.at[g, pl.ds(0, HALF)],
                               hsend.at[a, 0, g], hrecv.at[a, 0, g], nxt))
            mine.append(remote(src.at[pl.ds(0, HALF), cols], dst.at[g, pl.ds(3 * HALF, HALF)],
                               hsend.at[a, 1, g], hrecv.at[a, 1, g], prev))
        for cp in mine:
            cp.start()
        halos.append(mine)

    for cp in loads:
        cp.wait()

    row_j = lax.broadcasted_iota(jnp.int32, (HALF, 2 * HALF), 0)
    col_i = lax.broadcasted_iota(jnp.int32, (HALF, 2 * HALF), 1) % HALF
    keep = row_j >= col_i
    first_dev = jnp.where(me == 0, NEG, 0.0).astype(F32)
    last_dev = jnp.where(me == n_seq - 1, NEG, 0.0).astype(F32)
    bias[0] = jnp.where(keep, first_dev, 0.0)
    bias[1] = jnp.where(keep, 0.0, last_dev)
    lane = lax.broadcasted_iota(jnp.int32, (HALF, HALF), 1)
    left = lane < HEAD

    def stacked(t):
        zero = jnp.zeros_like(t)
        return jnp.concatenate([jnp.where(left, t, zero), jnp.where(left, zero, t)], axis=0)

    for g in range(GROUPS):
        dattn = dot(og[...], w_s[g * GW:(g + 1) * GW, :], NT).astype(BF).astype(F32)
        for p in range(2):
            for b in range(2):
                rb, cb = b * HALF, p * HALF
                d_st[g, p, b] = stacked(dattn[rb:rb + HALF, cb:cb + HALF]).astype(BF)
                qq = q_s[g, rb:rb + HALF, cb:cb + HALF].astype(F32) * SCALE
                q_st[g, p, b] = stacked(qq).astype(BF)
            k_t[g, p, :, HALF:3 * HALF] = k_s[g, HALF:3 * HALF, cb:cb + HALF].T
            v_t[g, p, :, HALF:3 * HALF] = v_s[g, HALF:3 * HALF, cb:cb + HALF].T

    def diagonal(t):
        return jnp.concatenate([t[:HEAD, :HALF], t[HEAD:, HALF:]], axis=0)

    def forward(g):
        for p in range(2):
            cb = p * HALF
            for e in (0, 3 * HALF):
                k_t[g, p, :, e:e + HALF] = k_s[g, e:e + HALF, cb:cb + HALF].T
                v_t[g, p, :, e:e + HALF] = v_s[g, e:e + HALF, cb:cb + HALF].T
            for b in range(2):
                r0 = b * HALF
                sc = dot(k_s[g, r0:r0 + 3 * HALF, cb:cb + HALF], q_st[g, p, b], NT)
                mid = sc[HALF:2 * HALF]
                mix = jnp.where(keep, sc[:HALF], sc[2 * HALF:]) + bias[b]
                top = jnp.maximum(jnp.max(mid, axis=0, keepdims=True),
                                  jnp.max(mix, axis=0, keepdims=True))
                mid = jnp.exp(mid - top)
                mix = jnp.exp(mix - top)
                total = jnp.sum(mid, axis=0, keepdims=True) + jnp.sum(mix, axis=0, keepdims=True)
                inv = 1.0 / total
                mid = mid * inv
                mix = mix * inv
                pr = jnp.concatenate(
                    [jnp.where(keep, mix, 0.0), mid, jnp.where(keep, 0.0, mix)], axis=0).astype(BF)
                p_s[g, p, b] = pr
                att = dot(v_t[g, p, :, r0:r0 + 3 * HALF], pr)
                a_t[cb:cb + HALF, r0:r0 + HALF] = diagonal(att).astype(BF)

    def project(g, slot):
        for h in range(NZ):
            r = dot(a_t[h * HEAD:(h + 1) * HEAD, :], og[...])
            part[slot, h * 8:(h + 1) * 8] = r.reshape(8, 8, r.shape[1])
        for yy in range(NY):
            for h in range(0, NZ, 2):
                t = jnp.concatenate([part[slot, h * 8 + yy * 2 + (1 - c)],
                                     part[slot, (h + 1) * 8 + yy * 2 + (1 - c)]], axis=0)
                r0 = yy * 32 + h * 8
                cs[slot, r0:r0 + 16] = t.astype(BF)
        cp = remote(cs.at[slot], cr.at[slot], csend.at[slot], crecv.at[slot], mate)
        cp.start()
        return cp

    def summed(slot, yy, h):
        r0 = yy * 32 + h * 8
        t = jnp.concatenate([part[slot, h * 8 + yy * 2 + c],
                             part[slot, (h + 1) * 8 + yy * 2 + c]], axis=0)
        return t + cr[slot, r0:r0 + 16].astype(F32)

    pieces = [(yy, h) for yy in range(NY) for h in range(0, NZ, 2)]

    def x_fill(slot, extra):
        for yy, h in pieces:
            r0 = yy * 32 + h * 8
            t = summed(slot, yy, h)
            if extra:
                t = t + xr[0, r0:r0 + 16].astype(F32)
            xs[slot, r0:r0 + 16] = t.astype(BF)

    far = remote(xs.at[0], xr.at[0], xsend.at[0], xrecv.at[0], x_far)
    up = remote(xs.at[1], xr.at[1], xsend.at[1], xrecv.at[1], x_up)
    down = remote(xs.at[2], xr.at[2], xsend.at[2], xrecv.at[2], x_dn)

    def x_send(slot):
        cores[slot].wait_recv()
        if slot == 0:
            x_fill(0, False)
            far.start()
            return
        adds = c == (0 if slot == 1 else 1)

        @pl.when(adds)
        def _():
            far.wait_recv()
            x_fill(slot, True)

        @pl.when(jnp.logical_not(adds))
        def _():
            x_fill(slot, False)

        (up if slot == 1 else down).start()

    cores = []
    for i, g in enumerate(order):
        for cp in halos[i]:
            cp.wait_recv()
        forward(g)
        cores.append(project(g, i))
        if i >= 1:
            x_send(i - 1)

    def backward(g):
        for p in range(2):
            cb = p * HALF
            dks, dvs = [], []
            for b in range(2):
                r0 = b * HALF
                dp = dot(v_s[g, r0:r0 + 3 * HALF, cb:cb + HALF], d_st[g, p, b], NT)
                pr = p_s[g, p, b]
                prf = pr.astype(F32)
                t = prf * dp
                delta = jnp.sum(t, axis=0, keepdims=True)
                ds = (t - prf * delta).astype(BF)
                dq = diagonal(dot(k_t[g, p, :, r0:r0 + 3 * HALF], ds)) * SCALE
                qo[r0:r0 + HALF, pl.ds(pl.multiple_of(g * GW + cb, HALF), HALF)] = dq.T.astype(BF)
                dks.append(dot(ds, q_st[g, p, b]))
                dvs.append(dot(pr, d_st[g, p, b]))
            for a, t in enumerate((dks, dvs)):
                rs[0, g, a, :, cb:cb + HALF] = t[0][:HALF].astype(BF)
                rs[1, g, a, :, cb:cb + HALF] = t[1][2 * HALF:].astype(BF)
                own[g, a, :HALF, cb:cb + HALF] = t[0][HALF:2 * HALF] + t[1][:HALF]
                own[g, a, HALF:, cb:cb + HALF] = t[0][2 * HALF:] + t[1][HALF:2 * HALF]
        lo = remote(rs.at[0, g], rr.at[0, g], rsend.at[0, g], rrecv.at[0, g], prev)
        hi = remote(rs.at[1, g], rr.at[1, g], rsend.at[1, g], rrecv.at[1, g], nxt)
        lo.start()
        hi.start()
        return lo, hi

    def finish(i):
        g = order[i]
        for cp in rims[i]:
            cp.wait_recv()
        cols = pl.ds(pl.multiple_of(g * GW, GW), GW)
        for a, out in enumerate((ko, vo)):
            out[:HALF, cols] = (own[g, a, :HALF] + rr[1, g, a].astype(F32)).astype(BF)
            out[HALF:, cols] = (own[g, a, HALF:] + rr[0, g, a].astype(F32)).astype(BF)

    y_copies = [remote(ysend.at[(y + i) % NY], yrecv.at[i - 1], ysem.at[i - 1], yrsem.at[i - 1],
                       y_to[i - 1]) for i in range(1, NY)]
    z_copies = [remote(zs.at[z], zr.at[i], zsem.at[i], zrsem.at[i], z_to[i][0], z_to[i][1])
                for i, z in enumerate(z_all)]

    def y_stage():
        cores[3].wait_recv()
        up.wait_recv()
        down.wait_recv()
        for yy, h in pieces:
            r0 = yy * 32 + h * 8
            t = (summed(3, yy, h) + xr[1, r0:r0 + 16].astype(F32)
                 + xr[2, r0:r0 + 16].astype(F32))
            ysend[yy, h * 8:h * 8 + 16] = t.astype(BF)
            part[0, h * 4 + yy] = t[:8]
            part[0, (h + 1) * 4 + yy] = t[8:]
        for cp in y_copies:
            cp.start()

    def z_stage():
        for cp in y_copies:
            cp.wait_recv()
        half = og.shape[1] // n_dp
        got = yrecv[0].astype(F32) + yrecv[1].astype(F32) + yrecv[2].astype(F32)
        for h in range(NZ):
            t = part[0, h * 4 + y] + got[h * 8:(h + 1) * 8]
            for d in range(n_dp):
                zs[d * NZ + h] = t[:, d * half:(d + 1) * half]
        for cp in z_copies:
            cp.start()

    def z_finish():
        for cp in z_copies:
            cp.wait_recv()
        t = zs[z_me]
        for i in range(len(z_copies)):
            t = t + zr[i]
        wo[...] = t * ((rows * n_seq * n_dp) ** -0.5)

    rims = []
    for i, g in enumerate(order):
        rims.append(backward(g))
        if i == 0:
            y_stage()
        elif i == 1:
            z_stage()
        elif i == 2:
            finish(0)
        else:
            z_finish()
            finish(1)
    finish(2)
    finish(3)

    for mine in halos:
        for cp in mine:
            cp.wait_send()
    for cp in cores + [far, up, down] + y_copies + z_copies:
        cp.wait_send()

    for mine in rims:
        for cp in mine:
            cp.wait_send()


def on_device(n_seq, n_dp, queries, keys, values, out_grad, out_weight):
    rows, width = queries.shape[1:]
    half = width // n_dp
    vm = pltpu.VMEM
    dma = pltpu.SemaphoreType.DMA
    nz = NZ * n_dp
    anyspec = pl.BlockSpec(memory_space=pl.ANY)
    vspec = pl.BlockSpec(memory_space=pltpu.VMEM)
    scratch = [
        vm((GROUPS, rows, GW), BF), vm((GROUPS, 4 * HALF, GW), BF), vm((GROUPS, 4 * HALF, GW), BF),
        vm((rows, width), BF), vm((width, width), BF),
        vm((GROUPS, 2, HALF, 4 * HALF), BF), vm((GROUPS, 2, HALF, 4 * HALF), BF),
        vm((GROUPS, 2, 2, 2 * HALF, HALF), BF), vm((GROUPS, 2, 2, 2 * HALF, HALF), BF),
        vm((GROUPS, 2, 2, 3 * HALF, 2 * HALF), BF), vm((GW, rows), BF), vm((2, HALF, 2 * HALF), F32),
        vm((4, 32, 8, width), F32), vm((4, HALF, width), BF), vm((4, HALF, width), BF),
        vm((3, HALF, width), BF), vm((3, HALF, width), BF),
        vm((NY, 32, width), BF), vm((NY - 1, 32, width), BF),
        vm((nz, 8, half), F32), vm((nz - 1, 8, half), F32),
        vm((2, GROUPS, 2, HALF, GW), BF), vm((2, GROUPS, 2, HALF, GW), BF),
        vm((GROUPS, 2, rows, GW), F32),
        dma((14,)), dma((2, 2, GROUPS)), dma((2, 2, GROUPS)), dma((4,)), dma((4,)),
        dma((3,)), dma((3,)), dma((NY - 1,)), dma((NY - 1,)), dma((nz - 1,)), dma((nz - 1,)),
        dma((2, GROUPS)), dma((2, GROUPS)),
    ]
    sds = jax.ShapeDtypeStruct
    qg, kg, vg, wg = pl.pallas_call(
        functools.partial(kernel, n_seq, n_dp),
        out_shape=[sds((rows, width), BF)] * 3 + [sds((8, half), F32)],
        in_specs=[anyspec] * 5,
        out_specs=[vspec] * 4,
        scratch_shapes=scratch,
        compiler_params=pltpu.CompilerParams(
            collective_id=0, has_side_effects=True, vmem_limit_bytes=48 * 1024 * 1024),
    )(queries[0], keys[0], values[0], out_grad[0], out_weight)
    return qg[None], kg[None], vg[None], wg


def solution(mesh):
    n_seq, n_dp = mesh.shape["seq"], mesh.shape["dp"]
    rows = P("dp", "seq", None)
    return jax.shard_map(
        functools.partial(on_device, n_seq, n_dp),
        mesh=mesh,
        in_specs=(rows, rows, rows, rows, P()),
        out_specs=(rows, rows, rows, P("seq", "dp")),
        check_vma=False,
    )
```

time: 814 us -> 63.8 us (0.08)
  the two profiles are of different devices: /device:TPU:96 before, /device:TPU:6 now
where the time goes in v1:
time: 63.8 us; the launch traced here: 63.5 us
  Pallas kernels  54.1 us (85%)
  local copies, waits for them, and re-layouts  8.73 us (14%)
  between operations  0.65 us (1%)
    pallas_call x1, Pallas kernels, on_device(): pl.pallas_call(functools.partial(kernel, n_seq, n_dp), out_shape=[sds((ro...  54.1 us
    unnamed x14, local copies, waits for them, and re-layouts  8.73 us

profile of v1, /device:TPU:6, one launch (start us, length us, event | category | flops | bytes accessed | tf_op | source)
XLA Modules:
  0.0 63.5 jit_solution(1810867351230044764)
XLA Ops:
  0.6 0.0 copy-start
  0.6 1.6 %copy-done = bf16[1024,1024]{1,0:T(8,128)(2,1)S(1)} copy-done((bf16[1024,1024]{1,0:T(8,128)(2,1)S(1)}, bf16[1024,1024]{1,0:T(8,128)(2,1)}, u32[]{:S(2)}) %copy-start) | copy-done | bytes 2097176
  2.2 0.0 copy-start.1
  2.2 1.0 %copy-done.1 = bf16[1,256,1024]{2,1,0:T(8,128)(2,1)S(1)} copy-done((bf16[1,256,1024]{2,1,0:T(8,128)(2,1)S(1)}, bf16[1,256,1024]{2,1,0:T(8,128)(2,1)}, u32[]{:S(2)}) %copy-start.1) | copy-done | bytes 524312
  3.3 0.0 copy-start.2
  3.3 1.0 %copy-done.2 = bf16[1,256,1024]{2,1,0:T(8,128)(2,1)S(1)} copy-done((bf16[1,256,1024]{2,1,0:T(8,128)(2,1)S(1)}, bf16[1,256,1024]{2,1,0:T(8,128)(2,1)}, u32[]{:S(2)}) %copy-start.2) | copy-done | bytes 524312
  4.3 0.0 copy-start.3
  4.3 1.0 %copy-done.3 = bf16[1,256,1024]{2,1,0:T(8,128)(2,1)S(1)} copy-done((bf16[1,256,1024]{2,1,0:T(8,128)(2,1)S(1)}, bf16[1,256,1024]{2,1,0:T(8,128)(2,1)}, u32[]{:S(2)}) %copy-start.3) | copy-done | bytes 524312
  5.4 0.0 copy-start.4
  5.4 1.0 %copy-done.4 = bf16[1,256,1024]{2,1,0:T(8,128)(2,1)S(1)} copy-done((bf16[1,256,1024]{2,1,0:T(8,128)(2,1)S(1)}, bf16[1,256,1024]{2,1,0:T(8,128)(2,1)}, u32[]{:S(2)}) %copy-start.4) | copy-done | bytes 524312
  6.4 54.1 %shard_map.84 = (bf16[256,1024]{1,0:T(8,128)(2,1)S(1)}, bf16[256,1024]{1,0:T(8,128)(2,1)S(1)}, bf16[256,1024]{1,0:T(8,128)(2,1)S(1)}, f32[8,512]{1,0:T(8,128)S(1)}) custom-call(bf16[256,1024]{1,0:T(8,128)(2,1)S(1)} %bitcast.10, bf16[256,1024]{1,0:T(8,128)(2,1)S(1)} %bitcast.11, bf16[256,1024]{1,0:T(8,128)(2,1)S(1)} %bitcast.12, ...), custom_call_target="tpu_custom_call" | custom-call | tf_op jit(solution)/shard_map/pallas_call | solution.py:339
  60.5 0.8 %copy.13 = bf16[1,256,1024]{2,1,0:T(8,128)(2,1)} copy(bf16[1,256,1024]{2,1,0:T(8,128)(2,1)S(1)} %bitcast.9) | data formatting | bytes 1048576
  61.3 0.8 %copy.14 = bf16[1,256,1024]{2,1,0:T(8,128)(2,1)} copy(bf16[1,256,1024]{2,1,0:T(8,128)(2,1)S(1)} %bitcast.8) | data formatting | bytes 1048576
  62.1 0.8 %copy.15 = bf16[1,256,1024]{2,1,0:T(8,128)(2,1)} copy(bf16[1,256,1024]{2,1,0:T(8,128)(2,1)S(1)} %bitcast.7) | data formatting | bytes 1048576
  62.9 0.6 copy.16
Async XLA Ops:
  0.6 1.6 %copy-start = (bf16[1024,1024]{1,0:T(8,128)(2,1)S(1)}, bf16[1024,1024]{1,0:T(8,128)(2,1)}, u32[]{:S(2)}) copy-start(bf16[1024,1024]{1,0:T(8,128)(2,1)} %w_h.1) | copy-start | bytes 6291460
  2.2 1.0 %copy-start.1 = (bf16[1,256,1024]{2,1,0:T(8,128)(2,1)S(1)}, bf16[1,256,1024]{2,1,0:T(8,128)(2,1)}, u32[]{:S(2)}) copy-start(bf16[1,256,1024]{2,1,0:T(8,128)(2,1)} %param.5) | copy-start | bytes 1572868
  3.3 1.0 %copy-start.2 = (bf16[1,256,1024]{2,1,0:T(8,128)(2,1)S(1)}, bf16[1,256,1024]{2,1,0:T(8,128)(2,1)}, u32[]{:S(2)}) copy-start(bf16[1,256,1024]{2,1,0:T(8,128)(2,1)} %param.6) | copy-start | bytes 1572868
  4.3 1.0 %copy-start.3 = (bf16[1,256,1024]{2,1,0:T(8,128)(2,1)S(1)}, bf16[1,256,1024]{2,1,0:T(8,128)(2,1)}, u32[]{:S(2)}) copy-start(bf16[1,256,1024]{2,1,0:T(8,128)(2,1)} %param.7) | copy-start | bytes 1572868
  5.4 1.0 %copy-start.4 = (bf16[1,256,1024]{2,1,0:T(8,128)(2,1)S(1)}, bf16[1,256,1024]{2,1,0:T(8,128)(2,1)}, u32[]{:S(2)}) copy-start(bf16[1,256,1024]{2,1,0:T(8,128)(2,1)} %param.8) | copy-start | bytes 1572868

commit v2 on v1

v2 whole, which is shorter than its diff:
```python
import functools

import jax
import jax.numpy as jnp
from jax import lax
from jax.experimental import pallas as pl
from jax.experimental.pallas import tpu as pltpu
from jax.sharding import PartitionSpec as P

HEAD = 64
HALF = 128
BF = jnp.bfloat16
F32 = jnp.float32
NEG = -1e30
NX, NZ, NY, NC = 4, 4, 4, 2
GROUPS = 4
GW = 256
NT = (((1,), (1,)), ((), ()))
NN = (((1,), (0,)), ((), ()))
SCALE = HEAD ** -0.5


def dot(a, b, dims=NN):
    return lax.dot_general(a, b, dims, preferred_element_type=F32)


def kernel(n_seq, n_dp, q_h, k_h, v_h, g_h, w_h, qo, ko, vo, wo,
           q_s, k_s, v_s, og, w_s, k_t, v_t, q_st, d_st, p_s, a_t, bias,
           part, cs, cr, xs, xr, ysend, yrecv, y_own, zs, zr, z_own, rs, rr, own,
           load_sem, hsend, hrecv, csend, crecv, xsend, xrecv, ysem, yrsem,
           zsem, zrsem, rsend, rrecv):
    me = lax.axis_index("seq")
    zh = lax.axis_index("dp")
    c = me % NC
    y = (me // NC) % NY
    zl = (me // (NC * NY)) % NZ
    x = me // (NC * NY * NZ)
    rows = 2 * HALF

    def at(x_, z_, y_, c_):
        return ((x_ * NZ + z_) * NY + y_) * NC + c_

    prev = (me + n_seq - 1) % n_seq
    nxt = (me + 1) % n_seq
    mate = at(x, zl, y, 1 - c)
    x_up = at((x + 1) % NX, zl, y, c)
    x_dn = at((x + NX - 1) % NX, zl, y, c)
    x_far = at((x + 1 + (NX - 2) * c) % NX, zl, y, c)
    y_to = [at(x, zl, (y + i) % NY, c) for i in range(1, NY)]
    z_me = zh * NZ + zl
    z_all = [(z_me + i) % (NZ * n_dp) for i in range(1, NZ * n_dp)]
    z_to = [(at(x, z % NZ, y, c), z // NZ) for z in z_all]

    def remote(src, dst, ss, rsem, seq, dp=None):
        return pltpu.make_async_remote_copy(
            src_ref=src, dst_ref=dst, send_sem=ss, recv_sem=rsem,
            device_id={"seq": seq, "dp": zh if dp is None else dp},
            device_id_type=pl.DeviceIdType.MESH)

    barrier = pltpu.get_barrier_semaphore()
    partners = [(prev, zh), (nxt, zh), (x_up, zh), (x_dn, zh)]
    partners += [(s, zh) for s in y_to] + z_to
    for s, d in partners:
        pl.semaphore_signal(barrier, inc=1, device_id={"seq": s, "dp": d},
                            device_id_type=pl.DeviceIdType.MESH)

    loads = [pltpu.make_async_copy(g_h, og, load_sem.at[0]),
             pltpu.make_async_copy(w_h, w_s, load_sem.at[1])]
    for g in range(GROUPS):
        cols = pl.ds(g * GW, GW)
        loads.append(pltpu.make_async_copy(q_h.at[:, cols], q_s.at[g], load_sem.at[2 + g]))
        loads.append(pltpu.make_async_copy(
            k_h.at[:, cols], k_s.at[g, pl.ds(HALF, rows)], load_sem.at[6 + g]))
        loads.append(pltpu.make_async_copy(
            v_h.at[:, cols], v_s.at[g, pl.ds(HALF, rows)], load_sem.at[10 + g]))
    for cp in loads:
        cp.start()

    pl.semaphore_wait(barrier, len(partners))

    def order_of(x_):
        return [(x_ + 2) % NX, (x_ + 1) % NX, (x_ + 3) % NX, x_]

    def halo(a, side, g):
        src, dst = ((k_h, k_s), (v_h, v_s))[a]
        cols = pl.ds(pl.multiple_of(g * GW, GW), GW)
        return remote(src.at[pl.ds(HALF * (1 - side), HALF), cols],
                      dst.at[g, pl.ds(3 * HALF * side, HALF)],
                      hsend.at[a, side, g], hrecv.at[a, side, g], (nxt, prev)[side])

    order = order_of(x)
    per_x = NZ * NY * NC
    for g_nxt, g_prev in zip(order_of(nxt // per_x), order_of(prev // per_x)):
        for a in range(2):
            halo(a, 0, g_nxt).start()
            halo(a, 1, g_prev).start()
    halos = [[halo(a, side, g) for a in range(2) for side in range(2)] for g in order]

    for cp in loads:
        cp.wait()

    row_j = lax.broadcasted_iota(jnp.int32, (HALF, 2 * HALF), 0)
    col_i = lax.broadcasted_iota(jnp.int32, (HALF, 2 * HALF), 1) % HALF
    keep = row_j >= col_i
    first_dev = jnp.where(me == 0, NEG, 0.0).astype(F32)
    last_dev = jnp.where(me == n_seq - 1, NEG, 0.0).astype(F32)
    bias[0] = jnp.where(keep, first_dev, 0.0)
    bias[1] = jnp.where(keep, 0.0, last_dev)
    lane = lax.broadcasted_iota(jnp.int32, (HALF, HALF), 1)
    left = lane < HEAD

    def stacked(t):
        zero = jnp.zeros_like(t)
        return jnp.concatenate([jnp.where(left, t, zero), jnp.where(left, zero, t)], axis=0)

    for g in range(GROUPS):
        dattn = dot(og[...], w_s[g * GW:(g + 1) * GW, :], NT).astype(BF).astype(F32)
        for p in range(2):
            cb = p * HALF
            for b in range(2):
                rb = b * HALF
                d_st[g, p, b] = stacked(dattn[rb:rb + HALF, cb:cb + HALF]).astype(BF)
                qq = q_s[g, rb:rb + HALF, cb:cb + HALF].astype(F32) * SCALE
                q_st[g, p, b] = stacked(qq).astype(BF)
            k_t[g, p, :, HALF:3 * HALF] = k_s[g, HALF:3 * HALF, cb:cb + HALF].T
            v_t[g, p, :, HALF:3 * HALF] = v_s[g, HALF:3 * HALF, cb:cb + HALF].T

    def diagonal(t):
        return jnp.concatenate([t[:HEAD, :HALF], t[HEAD:, HALF:]], axis=0)

    def forward(g, p):
        cb = p * HALF
        for e in (0, 3 * HALF):
            v_t[g, p, :, e:e + HALF] = v_s[g, e:e + HALF, cb:cb + HALF].T
        for b in range(2):
            r0 = b * HALF
            sc = dot(k_s[g, r0:r0 + 3 * HALF, cb:cb + HALF], q_st[g, p, b], NT)
            mid = sc[HALF:2 * HALF]
            mix = jnp.where(keep, sc[:HALF], sc[2 * HALF:]) + bias[b]
            top = jnp.maximum(jnp.max(mid, axis=0, keepdims=True),
                              jnp.max(mix, axis=0, keepdims=True))
            mid = jnp.exp(mid - top)
            mix = jnp.exp(mix - top)
            total = jnp.sum(mid, axis=0, keepdims=True) + jnp.sum(mix, axis=0, keepdims=True)
            inv = 1.0 / total
            mid = mid * inv
            mix = mix * inv
            pr = jnp.concatenate(
                [jnp.where(keep, mix, 0.0), mid, jnp.where(keep, 0.0, mix)], axis=0).astype(BF)
            p_s[g, p, b] = pr
            att = dot(v_t[g, p, :, r0:r0 + 3 * HALF], pr)
            a_t[:, r0:r0 + HALF] = diagonal(att).astype(BF)

    def project(slot):
        r = dot(a_t[...], og[...])
        part[slot] = r.reshape(16, 8, r.shape[1])
        for yy in range(NY):
            t = jnp.concatenate([part[slot, yy * 2 + (1 - c)],
                                 part[slot, 8 + yy * 2 + (1 - c)]], axis=0)
            cs[slot, yy * 16:yy * 16 + 16] = t.astype(BF)
        cp = remote(cs.at[slot], cr.at[slot], csend.at[slot], crecv.at[slot], mate)
        cp.start()
        return cp

    def summed(slot, yy):
        t = jnp.concatenate([part[slot, yy * 2 + c], part[slot, 8 + yy * 2 + c]], axis=0)
        return t + cr[slot, yy * 16:yy * 16 + 16].astype(F32)

    x_dest = [x_far, x_far, x_up, x_dn, x_up, x_dn]
    x_copies = [remote(xs.at[k], xr.at[k], xsend.at[k], xrecv.at[k], x_dest[k]) for k in range(6)]

    def x_fill(slot, extra):
        for yy in range(NY):
            t = summed(slot, yy)
            if extra is not None:
                t = t + xr[extra, yy * 16:yy * 16 + 16].astype(F32)
            xs[slot, yy * 16:yy * 16 + 16] = t.astype(BF)

    def x_send(slot):
        cores[slot].wait_recv()
        if slot < 2:
            x_fill(slot, None)
        else:
            far = 0 if slot < 4 else 1
            adds = c == slot % 2

            @pl.when(adds)
            def _():
                x_copies[far].wait_recv()
                x_fill(slot, far)

            @pl.when(jnp.logical_not(adds))
            def _():
                x_fill(slot, None)

        x_copies[slot].start()

    cores = []
    g_far, g_up, g_dn, g_own = order
    steps = [(0, g_far, 0), (0, g_far, 1), (1, g_up, 0), (2, g_dn, 0),
             (1, g_up, 1), (2, g_dn, 1), (3, g_own, 0), (3, g_own, 1)]
    x_after = {1: [0], 2: [1], 4: [2, 3], 5: [4], 6: [5]}
    for i, (place, g, p) in enumerate(steps):
        if i in (0, 2, 3, 6):
            for cp in halos[place]:
                cp.wait_recv()
        forward(g, p)
        cores.append(project(i))
        for slot in x_after.get(i, []):
            x_send(slot)

    def backward(g, p):
        cb = p * HALF
        for e in (0, 3 * HALF):
            k_t[g, p, :, e:e + HALF] = k_s[g, e:e + HALF, cb:cb + HALF].T
        dks, dvs = [], []
        for b in range(2):
            r0 = b * HALF
            dp = dot(v_s[g, r0:r0 + 3 * HALF, cb:cb + HALF], d_st[g, p, b], NT)
            pr = p_s[g, p, b]
            prf = pr.astype(F32)
            t = prf * dp
            delta = jnp.sum(t, axis=0, keepdims=True)
            ds = (t - prf * delta).astype(BF)
            dks.append(dot(ds, q_st[g, p, b]))
            dvs.append(dot(pr, d_st[g, p, b]))
            dq = diagonal(dot(k_t[g, p, :, r0:r0 + 3 * HALF], ds)) * SCALE
            qo[r0:r0 + HALF, g * GW + cb:g * GW + cb + HALF] = dq.T.astype(BF)
        j = g * 2 + p
        for a, t in enumerate((dks, dvs)):
            rs[0, j, a] = t[0][:HALF].astype(BF)
            rs[1, j, a] = t[1][2 * HALF:].astype(BF)
            own[j, a, :HALF] = t[0][HALF:2 * HALF] + t[1][:HALF]
            own[j, a, HALF:] = t[0][2 * HALF:] + t[1][HALF:2 * HALF]
        lo = remote(rs.at[0, j], rr.at[0, j], rsend.at[0, j], rrecv.at[0, j], prev)
        hi = remote(rs.at[1, j], rr.at[1, j], rsend.at[1, j], rrecv.at[1, j], nxt)
        lo.start()
        hi.start()
        return lo, hi

    def finish(j):
        for cp in rims[j]:
            cp.wait_recv()
        for a, out in enumerate((ko, vo)):
            cols = slice(j * HALF, (j + 1) * HALF)
            out[:HALF, cols] = (own[j, a, :HALF] + rr[1, j, a].astype(F32)).astype(BF)
            out[HALF:, cols] = (own[j, a, HALF:] + rr[0, j, a].astype(F32)).astype(BF)

    y_copies = [[remote(ysend.at[p, (y + i) % NY], yrecv.at[p, i - 1], ysem.at[p, i - 1],
                        yrsem.at[p, i - 1], y_to[i - 1]) for i in range(1, NY)] for p in range(2)]
    z_copies = [remote(zs.at[z], zr.at[i], zsem.at[i], zrsem.at[i], z_to[i][0], z_to[i][1])
                for i, z in enumerate(z_all)]
    quarter = og.shape[1] // (2 * n_dp)

    def y_stage(p):
        cores[6 + p].wait_recv()
        x_copies[2 + 2 * p].wait_recv()
        x_copies[3 + 2 * p].wait_recv()
        for yy in range(NY):
            r0 = yy * 16
            t = (summed(6 + p, yy) + xr[2 + 2 * p, r0:r0 + 16].astype(F32)
                 + xr[3 + 2 * p, r0:r0 + 16].astype(F32))
            ysend[p, yy] = t.astype(BF)
            y_own[p, yy] = t
        for cp in y_copies[p]:
            cp.start()

    def z_stage():
        for p in range(2):
            for cp in y_copies[p]:
                cp.wait_recv()
        for p in range(2):
            t = y_own[p, y]
            for i in range(NY - 1):
                t = t + yrecv[p, i].astype(F32)
            for h in range(2):
                for d in range(n_dp):
                    u = t[h * 8:h * 8 + 8, d * 2 * quarter:(d + 1) * 2 * quarter]
                    u = jnp.concatenate([u[:, :quarter], u[:, quarter:]], axis=0)
                    z_own[d * NZ + p * 2 + h] = u
                    zs[d * NZ + p * 2 + h] = u.astype(BF)
        for cp in z_copies:
            cp.start()

    def z_finish():
        for cp in z_copies:
            cp.wait_recv()
        t = z_own[z_me]
        for i in range(len(z_copies)):
            t = t + zr[i].astype(F32)
        t = t * ((rows * n_seq * n_dp) ** -0.5)
        wo[:, :quarter] = t[:8]
        wo[:, quarter:] = t[8:]

    rims = []
    for g in range(GROUPS):
        for p in range(2):
            rims.append(backward(g, p))
            if len(rims) == 3:
                y_stage(0)
            elif len(rims) == 5:
                y_stage(1)
    z_stage()
    for j in range(2 * GROUPS):
        finish(j)
    z_finish()

    for g_nxt, g_prev in zip(order_of(nxt // per_x), order_of(prev // per_x)):
        for a in range(2):
            halo(a, 0, g_nxt).wait_send()
            halo(a, 1, g_prev).wait_send()
    for cp in cores + x_copies + y_copies[0] + y_copies[1] + z_copies:
        cp.wait_send()
    for pair in rims:
        for cp in pair:
            cp.wait_send()


def on_device(n_seq, n_dp, queries, keys, values, out_grad, out_weight):
    rows, width = queries.shape[1:]
    half = width // n_dp
    vm = pltpu.VMEM
    dma = pltpu.SemaphoreType.DMA
    nz = NZ * n_dp
    anyspec = pl.BlockSpec(memory_space=pltpu.HBM)
    vspec = pl.BlockSpec(memory_space=pltpu.VMEM)
    scratch = [
        vm((GROUPS, rows, GW), BF), vm((GROUPS, 4 * HALF, GW), BF), vm((GROUPS, 4 * HALF, GW), BF),
        vm((rows, width), BF), vm((width, width), BF),
        vm((GROUPS, 2, HALF, 4 * HALF), BF), vm((GROUPS, 2, HALF, 4 * HALF), BF),
        vm((GROUPS, 2, 2, 2 * HALF, HALF), BF), vm((GROUPS, 2, 2, 2 * HALF, HALF), BF),
        vm((GROUPS, 2, 2, 3 * HALF, 2 * HALF), BF), vm((HALF, rows), BF), vm((2, HALF, 2 * HALF), F32),
        vm((8, 16, 8, width), F32), vm((8, HEAD, width), BF), vm((8, HEAD, width), BF),
        vm((6, HEAD, width), BF), vm((6, HEAD, width), BF),
        vm((2, NY, 16, width), BF), vm((2, NY - 1, 16, width), BF), vm((2, NY, 16, width), F32),
        vm((nz, 16, half // 2), BF), vm((nz - 1, 16, half // 2), BF), vm((nz, 16, half // 2), F32),
        vm((2, 8, 2, HALF, HALF), BF), vm((2, 8, 2, HALF, HALF), BF),
        vm((8, 2, rows, HALF), F32),
        dma((14,)), dma((2, 2, GROUPS)), dma((2, 2, GROUPS)), dma((8,)), dma((8,)),
        dma((6,)), dma((6,)), dma((2, NY - 1)), dma((2, NY - 1)), dma((nz - 1,)), dma((nz - 1,)),
        dma((2, 8)), dma((2, 8)),
    ]
    sds = jax.ShapeDtypeStruct
    outs = [sds((rows, width), BF)] * 3 + [sds((8, half), F32)]
    qg, kg, vg, wg = pl.pallas_call(
        functools.partial(kernel, n_seq, n_dp),
        out_shape=outs,
        in_specs=[anyspec] * 5,
        out_specs=[vspec] * 4,
        scratch_shapes=scratch,
        compiler_params=pltpu.CompilerParams(
            collective_id=0, has_side_effects=True, vmem_limit_bytes=48 * 1024 * 1024),
    )(*[pltpu.with_memory_space_constraint(t, pltpu.HBM)
        for t in (queries[0], keys[0], values[0], out_grad[0], out_weight)])
    return qg[None], kg[None], vg[None], wg


def solution(mesh):
    n_seq, n_dp = mesh.shape["seq"], mesh.shape["dp"]
    rows = P("dp", "seq", None)
    return jax.shard_map(
        functools.partial(on_device, n_seq, n_dp),
        mesh=mesh,
        in_specs=(rows, rows, rows, rows, P()),
        out_specs=(rows, rows, rows, P("seq", "dp")),
        check_vma=False,
    )
```

time: 63.8 us -> 46.7 us (0.73)
  the two profiles are of different devices: /device:TPU:6 before, /device:TPU:1 now
where the time goes in v2:
time: 46.7 us
  Pallas kernels  43 us (92%)
  local copies, waits for them, and re-layouts  2.99 us (6%)
  between operations  0.64 us (1%)
    pallas_call x1, Pallas kernels, on_device(): pl.pallas_call(functools.partial(kernel, n_seq, n_dp), out_shape=outs, in...  43 us
    unnamed x4, local copies, waits for them, and re-layouts  2.99 us

profile of v2, /device:TPU:1, one launch (start us, length us, event | category | flops | bytes accessed | tf_op | source)
XLA Modules:
  0.0 46.7 jit_solution(150042215567384541)
XLA Ops:
  0.6 43.0 %shard_map.84 = (bf16[256,1024]{1,0:T(8,128)(2,1)S(1)}, bf16[256,1024]{1,0:T(8,128)(2,1)S(1)}, bf16[256,1024]{1,0:T(8,128)(2,1)S(1)}, f32[8,512]{1,0:T(8,128)S(1)}) custom-call(bf16[256,1024]{1,0:T(8,128)(2,1)} %bitcast.10, bf16[256,1024]{1,0:T(8,128)(2,1)} %bitcast.11, bf16[256,1024]{1,0:T(8,128)(2,1)} %bitcast.12, bf16[256,1024]{1,0:T(8,128)(2,1)} %bitcast.13, ...), custom_call_target="tpu_custom_call" | custom-call | tf_op jit(solution)/shard_map/pallas_call | solution.py:345
  43.7 0.8 %copy.13 = bf16[1,256,1024]{2,1,0:T(8,128)(2,1)} copy(bf16[1,256,1024]{2,1,0:T(8,128)(2,1)S(1)} %bitcast.9) | data formatting | bytes 1048576
  44.5 0.8 %copy.14 = bf16[1,256,1024]{2,1,0:T(8,128)(2,1)} copy(bf16[1,256,1024]{2,1,0:T(8,128)(2,1)S(1)} %bitcast.8) | data formatting | bytes 1048576
  45.3 0.8 %copy.15 = bf16[1,256,1024]{2,1,0:T(8,128)(2,1)} copy(bf16[1,256,1024]{2,1,0:T(8,128)(2,1)S(1)} %bitcast.7) | data formatting | bytes 1048576
  46.1 0.6 %copy.16 = f32[8,512]{1,0:T(8,128)} copy(f32[8,512]{1,0:T(8,128)S(1)} %get-tuple-element.19) | data formatting | bytes 32768

commit v3 on v2

v3 whole, which is shorter than its diff:
```python
import functools

import jax
import jax.numpy as jnp
from jax import lax
from jax.experimental import pallas as pl
from jax.experimental.pallas import tpu as pltpu
from jax.sharding import PartitionSpec as P

HEAD = 64
HALF = 128
BF = jnp.bfloat16
F32 = jnp.float32
NEG = -1e30
NX, NZ, NY, NC = 4, 4, 4, 2
GROUPS = 4
GW = 256
NT = (((1,), (1,)), ((), ()))
NN = (((1,), (0,)), ((), ()))
SCALE = HEAD ** -0.5


def dot(a, b, dims=NN):
    return lax.dot_general(a, b, dims, preferred_element_type=F32)


def kernel(n_seq, n_dp, q_h, k_h, v_h, g_h, w_h, all_o, wo,
           q_s, k_s, v_s, og, w_s, k_t, v_t, q_st, d_st, p_s, a_t, bias,
           part, cs, cr, xs, xr, ysend, yrecv, y_own, zs, zr, z_own, rs, rr, own,
           load_sem, hsend, hrecv, csend, crecv, xsend, xrecv, ysem, yrsem,
           zsem, zrsem, rsend, rrecv):
    me = lax.axis_index("seq")
    zh = lax.axis_index("dp")
    c = me % NC
    y = (me // NC) % NY
    zl = (me // (NC * NY)) % NZ
    x = me // (NC * NY * NZ)
    rows = 2 * HALF
    qo, ko, vo = all_o.at[0], all_o.at[1], all_o.at[2]

    def at(x_, z_, y_, c_):
        return ((x_ * NZ + z_) * NY + y_) * NC + c_

    prev = (me + n_seq - 1) % n_seq
    nxt = (me + 1) % n_seq
    mate = at(x, zl, y, 1 - c)
    x_up = at((x + 1) % NX, zl, y, c)
    x_dn = at((x + NX - 1) % NX, zl, y, c)
    x_far = at((x + 1 + (NX - 2) * c) % NX, zl, y, c)
    y_to = [at(x, zl, (y + i) % NY, c) for i in range(1, NY)]
    z_me = zh * NZ + zl
    z_all = [(z_me + i) % (NZ * n_dp) for i in range(1, NZ * n_dp)]
    z_to = [(at(x, z % NZ, y, c), z // NZ) for z in z_all]

    def remote(src, dst, ss, rsem, seq, dp=None):
        return pltpu.make_async_remote_copy(
            src_ref=src, dst_ref=dst, send_sem=ss, recv_sem=rsem,
            device_id={"seq": seq, "dp": zh if dp is None else dp},
            device_id_type=pl.DeviceIdType.MESH)

    barrier = pltpu.get_barrier_semaphore()
    partners = [(prev, zh), (nxt, zh), (x_up, zh), (x_dn, zh)]
    partners += [(s, zh) for s in y_to] + z_to
    for s, d in partners:
        pl.semaphore_signal(barrier, inc=1, device_id={"seq": s, "dp": d},
                            device_id_type=pl.DeviceIdType.MESH)

    def order_of(x_):
        return [(x_ + 2) % NX, (x_ + 1) % NX, (x_ + 3) % NX, x_]

    order = order_of(x)

    def loads(g):
        cols = pl.ds(pl.multiple_of(g * GW, GW), GW)
        mid = pl.ds(HALF, rows)
        return [pltpu.make_async_copy(q_h.at[:, cols], q_s.at[g], load_sem.at[2 + g]),
                pltpu.make_async_copy(k_h.at[:, cols], k_s.at[g, mid], load_sem.at[6 + g]),
                pltpu.make_async_copy(v_h.at[:, cols], v_s.at[g, mid], load_sem.at[10 + g])]

    load_og = pltpu.make_async_copy(g_h, og, load_sem.at[0])
    load_w = pltpu.make_async_copy(w_h, w_s, load_sem.at[1])
    for i, g in enumerate(order):
        for cp in loads(g):
            cp.start()
        if i == 0:
            load_og.start()
    load_w.start()

    pl.semaphore_wait(barrier, len(partners))

    away = (me + n_seq - 1 + 2 * c) % n_seq
    sides = ((mate, 1 - c), (away, c))

    def halo(a, side, g):
        buf = (k_s, v_s)[a]
        dev, b = sides[side]
        return remote(buf.at[g, pl.ds(pl.multiple_of(HALF * (1 + b), HALF), HALF)],
                      buf.at[g, pl.ds(pl.multiple_of(3 * HALF * (1 - b), HALF), HALF)],
                      hsend.at[a, side, g], hrecv.at[a, side, g], dev)

    away_order = order_of(away // (NZ * NY * NC))
    for g in order:
        for cp in loads(g)[1:]:
            cp.wait()
    for i in range(GROUPS):
        for a in range(2):
            halo(a, 1, away_order[i]).start()
            halo(a, 0, order[i]).start()

    row_j = lax.broadcasted_iota(jnp.int32, (HALF, 2 * HALF), 0)
    col_i = lax.broadcasted_iota(jnp.int32, (HALF, 2 * HALF), 1) % HALF
    keep = row_j >= col_i
    first_dev = jnp.where(me == 0, NEG, 0.0).astype(F32)
    last_dev = jnp.where(me == n_seq - 1, NEG, 0.0).astype(F32)
    bias[0] = jnp.where(keep, first_dev, 0.0)
    bias[1] = jnp.where(keep, 0.0, last_dev)
    lane = lax.broadcasted_iota(jnp.int32, (HALF, HALF), 1)
    left = lane < HEAD

    def stacked(t):
        zero = jnp.zeros_like(t)
        return jnp.concatenate([jnp.where(left, t, zero), jnp.where(left, zero, t)], axis=0)

    def diagonal(t):
        return jnp.concatenate([t[:HEAD, :HALF], t[HEAD:, HALF:]], axis=0)

    def block_rows(b):
        return pl.ds(pl.multiple_of(b * HALF, HALF), 3 * HALF)

    def edge_rows(b):
        return pl.ds(pl.multiple_of(b * 3 * HALF, HALF), HALF)

    def ready(g):
        loads(g)[0].wait()
        for p in range(2):
            cb = p * HALF
            for b in range(2):
                rb = b * HALF
                qq = q_s[g, rb:rb + HALF, cb:cb + HALF].astype(F32) * SCALE
                q_st[g, p, b] = stacked(qq).astype(BF)
            v_t[g, p, :, HALF:3 * HALF] = v_s[g, HALF:3 * HALF, cb:cb + HALF].T

    def forward(i, g, p, b):
        cb = p * HALF
        edge = edge_rows(b)
        rr0 = block_rows(b)
        v_t[g, p, :, edge] = v_s[g, edge, cb:cb + HALF].T
        sc = dot(k_s[g, rr0, cb:cb + HALF], q_st[g, p, b], NT)
        mid = sc[HALF:2 * HALF]
        mix = jnp.where(keep, sc[:HALF], sc[2 * HALF:]) + bias[b]
        top = jnp.maximum(jnp.max(mid, axis=0, keepdims=True),
                          jnp.max(mix, axis=0, keepdims=True))
        mid = jnp.exp(mid - top)
        mix = jnp.exp(mix - top)
        total = jnp.sum(mid, axis=0, keepdims=True) + jnp.sum(mix, axis=0, keepdims=True)
        inv = 1.0 / total
        mid = mid * inv
        mix = mix * inv
        pr = jnp.concatenate(
            [jnp.where(keep, mix, 0.0), mid, jnp.where(keep, 0.0, mix)], axis=0).astype(BF)
        p_s[g, p, b] = pr
        att = dot(v_t[g, p, :, rr0], pr)
        a_t[i, :, pl.ds(pl.multiple_of(b * HALF, HALF), HALF)] = diagonal(att).astype(BF)

    def project(slot):
        r = dot(a_t[slot], og[...])
        part[slot] = r.reshape(16, 8, r.shape[1])
        for yy in range(NY):
            t = jnp.concatenate([part[slot, yy * 2 + (1 - c)],
                                 part[slot, 8 + yy * 2 + (1 - c)]], axis=0)
            cs[slot, yy * 16:yy * 16 + 16] = t.astype(BF)
        cp = remote(cs.at[slot], cr.at[slot], csend.at[slot], crecv.at[slot], mate)
        cp.start()
        return cp

    def summed(slot, yy):
        t = jnp.concatenate([part[slot, yy * 2 + c], part[slot, 8 + yy * 2 + c]], axis=0)
        return t + cr[slot, yy * 16:yy * 16 + 16].astype(F32)

    x_dest = [x_far, x_far, x_up, x_dn, x_up, x_dn]
    x_copies = [remote(xs.at[k], xr.at[k], xsend.at[k], xrecv.at[k], x_dest[k]) for k in range(6)]

    def x_fill(slot, extra):
        for yy in range(NY):
            t = summed(slot, yy)
            if extra is not None:
                t = t + xr[extra, yy * 16:yy * 16 + 16].astype(F32)
            xs[slot, yy * 16:yy * 16 + 16] = t.astype(BF)

    def x_send(slot):
        cores[slot].wait_recv()
        if slot < 2:
            x_fill(slot, None)
        else:
            far = 0 if slot < 4 else 1
            adds = c == slot % 2

            @pl.when(adds)
            def _():
                x_copies[far].wait_recv()
                x_fill(slot, far)

            @pl.when(jnp.logical_not(adds))
            def _():
                x_fill(slot, None)

        x_copies[slot].start()

    cores = []
    g_far, g_up, g_dn, g_own = order
    steps = [(0, g_far, 0), (0, g_far, 1), (1, g_up, 0), (2, g_dn, 0),
             (1, g_up, 1), (2, g_dn, 1), (3, g_own, 0), (3, g_own, 1)]
    x_after = {1: [0], 2: [1], 5: [2, 3], 6: [4], 7: [5]}

    def near_step(i):
        place, g, p = steps[i]
        if i in (0, 2, 3, 6):
            ready(g)
            for a in range(2):
                halo(a, 0, g).wait_recv()
        forward(i, g, p, 1 - c)

    def away_step(i):
        place, g, p = steps[i]
        if i in (0, 2, 3, 6):
            for a in range(2):
                halo(a, 1, g).wait_recv()
        forward(i, g, p, c)
        cores.append(project(i))
        for slot in x_after.get(i, []):
            x_send(slot)

    def dattn_of(g):
        d = dot(og[...], w_s[g * GW:(g + 1) * GW, :], NT).astype(BF).astype(F32)
        for p in range(2):
            for b in range(2):
                d_st[g, p, b] = stacked(
                    d[b * HALF:(b + 1) * HALF, p * HALF:(p + 1) * HALF]).astype(BF)

    for i in range(len(steps)):
        near_step(i)
        if i == 1:
            load_og.wait()
            load_w.wait()
        if i % 2:
            dattn_of(i // 2)
    for i in range(len(steps)):
        away_step(i)

    def backward(g, p, side):
        dev, b = sides[side]
        cb = p * HALF
        j = g * 2 + p
        edge = edge_rows(b)
        rr0 = block_rows(b)
        if side == 1:
            k_t[g, p, :, HALF:3 * HALF] = k_s[g, HALF:3 * HALF, cb:cb + HALF].T
        k_t[g, p, :, edge] = k_s[g, edge, cb:cb + HALF].T
        dp = dot(v_s[g, rr0, cb:cb + HALF], d_st[g, p, b], NT)
        pr = p_s[g, p, b]
        prf = pr.astype(F32)
        t = prf * dp
        delta = jnp.sum(t, axis=0, keepdims=True)
        ds = (t - prf * delta).astype(BF)
        own[side, j, 0, rr0] = dot(ds, q_st[g, p, b])
        own[side, j, 1, rr0] = dot(pr, d_st[g, p, b])
        for a in range(2):
            rs[side, j, a] = own[side, j, a, edge].astype(BF)
        cp = remote(rs.at[side, j], rr.at[side, j], rsend.at[side, j], rrecv.at[side, j], dev)
        cp.start()
        dq = diagonal(dot(k_t[g, p, :, rr0], ds)) * SCALE
        qo[pl.ds(pl.multiple_of(b * HALF, HALF), HALF), j * HALF:(j + 1) * HALF] = dq.T.astype(BF)
        return cp

    def finish(j):
        for cp in (near_rims[j], away_rims[j]):
            cp.wait_recv()
        for a, out in enumerate((ko, vo)):
            for side in range(2):
                b = sides[side][1]
                r_in = pl.ds(pl.multiple_of((b + 1) * HALF, HALF), HALF)
                t = own[0, j, a, r_in] + own[1, j, a, r_in] + rr[side, j, a].astype(F32)
                out[pl.ds(pl.multiple_of(b * HALF, HALF), HALF),
                    j * HALF:(j + 1) * HALF] = t.astype(BF)

    quarter = og.shape[1] // (2 * n_dp)
    y_copies = [remote(ysend.at[(y + i) % NY], yrecv.at[i - 1], ysem.at[i - 1],
                       yrsem.at[i - 1], y_to[i - 1]) for i in range(1, NY)]

    def z_copy(to, frm):
        return remote(zs.at[to], zr.at[frm], zsem.at[to], zrsem.at[frm],
                      at(x, to % NZ, y, c), to // NZ)

    def z_stage(p):
        cores[6 + p].wait_recv()
        x_copies[2 + 2 * p].wait_recv()
        x_copies[3 + 2 * p].wait_recv()
        for yy in range(NY):
            r0 = yy * 16
            t = (summed(6 + p, yy) + xr[2 + 2 * p, r0:r0 + 16].astype(F32)
                 + xr[3 + 2 * p, r0:r0 + 16].astype(F32))
            for h in range(2):
                for d in range(n_dp):
                    u = t[h * 8:h * 8 + 8, d * 2 * quarter:(d + 1) * 2 * quarter]
                    u = jnp.concatenate([u[:, :quarter], u[:, quarter:]], axis=0)
                    z_own[d * NZ + p * 2 + h, r0:r0 + 16] = u
                    zs[d * NZ + p * 2 + h, r0:r0 + 16] = u.astype(BF)
        for h in range(2):
            for d in range(n_dp):
                to = d * NZ + p * 2 + h

                @pl.when(z_me != to)
                def _(to=to):
                    z_copy(to, z_me).start()

    def y_stage():
        for z in z_all:
            z_copy(z, z).wait_recv()
        for yy in range(NY):
            r0 = yy * 16
            t = z_own[z_me, r0:r0 + 16]
            for z in z_all:
                t = t + zr[z, r0:r0 + 16].astype(F32)
            y_own[yy] = t
            ysend[yy] = t.astype(BF)
        for cp in y_copies:
            cp.start()

    def y_finish():
        for cp in y_copies:
            cp.wait_recv()
        t = y_own[y]
        for i in range(NY - 1):
            t = t + yrecv[i].astype(F32)
        t = t * ((rows * n_seq * n_dp) ** -0.5)
        wo[:, :quarter] = t[:8]
        wo[:, quarter:] = t[8:]

    away_rims, near_rims = [], []
    for j in range(2 * GROUPS):
        away_rims.append(backward(j // 2, j % 2, 1))
    for j in range(2 * GROUPS):
        near_rims.append(backward(j // 2, j % 2, 0))
        if j == 1:
            z_stage(0)
        elif j == 6:
            z_stage(1)
    y_stage()
    for j in range(2 * GROUPS):
        finish(j)
    y_finish()

    for g in range(GROUPS):
        for a in range(2):
            for side in range(2):
                halo(a, side, g).wait_send()
    for cp in cores + x_copies + y_copies + [z_copy(z, z) for z in z_all]:
        cp.wait_send()
    for cp in away_rims + near_rims:
        cp.wait_send()


def on_device(n_seq, n_dp, queries, keys, values, out_grad, out_weight):
    rows, width = queries.shape[1:]
    half = width // n_dp
    vm = pltpu.VMEM
    dma = pltpu.SemaphoreType.DMA
    nz = NZ * n_dp
    anyspec = pl.BlockSpec(memory_space=pltpu.HBM)
    vspec = pl.BlockSpec(memory_space=pltpu.VMEM)
    scratch = [
        vm((GROUPS, rows, GW), BF), vm((GROUPS, 4 * HALF, GW), BF), vm((GROUPS, 4 * HALF, GW), BF),
        vm((rows, width), BF), vm((width, width), BF),
        vm((GROUPS, 2, HALF, 4 * HALF), BF), vm((GROUPS, 2, HALF, 4 * HALF), BF),
        vm((GROUPS, 2, 2, 2 * HALF, HALF), BF), vm((GROUPS, 2, 2, 2 * HALF, HALF), BF),
        vm((GROUPS, 2, 2, 3 * HALF, 2 * HALF), BF), vm((8, HALF, rows), BF), vm((2, HALF, 2 * HALF), F32),
        vm((8, 16, 8, width), F32), vm((8, HEAD, width), BF), vm((8, HEAD, width), BF),
        vm((6, HEAD, width), BF), vm((6, HEAD, width), BF),
        vm((NY, 16, half // 2), BF), vm((NY - 1, 16, half // 2), BF), vm((NY, 16, half // 2), F32),
        vm((nz, HEAD, half // 2), BF), vm((nz, HEAD, half // 2), BF), vm((nz, HEAD, half // 2), F32),
        vm((2, 8, 2, HALF, HALF), BF), vm((2, 8, 2, HALF, HALF), BF),
        vm((2, 8, 2, 4 * HALF, HALF), F32),
        dma((14,)), dma((2, 2, GROUPS)), dma((2, 2, GROUPS)), dma((8,)), dma((8,)),
        dma((6,)), dma((6,)), dma((NY - 1,)), dma((NY - 1,)), dma((nz,)), dma((nz,)),
        dma((2, 8)), dma((2, 8)),
    ]
    sds = jax.ShapeDtypeStruct
    outs = [sds((3, rows, width), BF), sds((8, half), F32)]
    qkv, wg = pl.pallas_call(
        functools.partial(kernel, n_seq, n_dp),
        out_shape=outs,
        in_specs=[anyspec] * 5,
        out_specs=[vspec] * 2,
        scratch_shapes=scratch,
        compiler_params=pltpu.CompilerParams(
            collective_id=0, has_side_effects=True, vmem_limit_bytes=48 * 1024 * 1024),
    )(*[pltpu.with_memory_space_constraint(t, pltpu.HBM)
        for t in (queries[0], keys[0], values[0], out_grad[0], out_weight)])
    return qkv[0:1], qkv[1:2], qkv[2:3], wg


def solution(mesh):
    n_seq, n_dp = mesh.shape["seq"], mesh.shape["dp"]
    rows = P("dp", "seq", None)
    return jax.shard_map(
        functools.partial(on_device, n_seq, n_dp),
        mesh=mesh,
        in_specs=(rows, rows, rows, rows, P()),
        out_specs=(rows, rows, rows, P("seq", "dp")),
        check_vma=False,
    )
```

time: 46.7 us -> 45.1 us (0.966)
  the two profiles are of different devices: /device:TPU:1 before, /device:TPU:96 now
where the time goes in v3:
time: 45.1 us; the launch traced here: 45 us
  Pallas kernels  42.6 us (94%)
  local copies, waits for them, and re-layouts  1.78 us (4%)
  between operations  0.64 us (1%)
    pallas_call x1, Pallas kernels, on_device(): pl.pallas_call(functools.partial(kernel, n_seq, n_dp), out_shape=outs, in...  42.6 us
    slice x1, local copies, waits for them, and re-layouts, on_device(): return (qkv[0:1], qkv[1:2], qkv[2:3], wg)  1.17 us

profile of v3, /device:TPU:96, one launch (start us, length us, event | category | flops | bytes accessed | tf_op | source)
XLA Modules:
  0.0 45.0 jit_solution(9890038086885613)
XLA Ops:
  0.6 42.6 %shard_map.84 = (bf16[3,256,1024]{2,1,0:T(8,128)(2,1)S(1)}, f32[8,512]{1,0:T(8,128)S(1)}) custom-call(bf16[256,1024]{1,0:T(8,128)(2,1)} %bitcast.4, bf16[256,1024]{1,0:T(8,128)(2,1)} %bitcast.5, bf16[256,1024]{1,0:T(8,128)(2,1)} %bitcast.6, bf16[256,1024]{1,0:T(8,128)(2,1)} %bitcast.7, bf16[1024,1024]{1,0:T(8,128)(2,1)} %w_h.1), custom_call_target="tpu_custom_call" | custom-call | tf_op jit(solution)/shard_map/pallas_call | solution.py:389
  43.2 1.2 %fusion = (bf16[1,256,1024]{2,1,0:T(8,128)(2,1)}, bf16[1,256,1024]{2,1,0:T(8,128)(2,1)}, bf16[1,256,1024]{2,1,0:T(8,128)(2,1)}) fusion(bf16[3,256,1024]{2,1,0:T(8,128)(2,1)S(1)} %get-tuple-element.6), kind=kLoop, calls=%fused_computation | loop fusion | bytes 3145728 | tf_op jit(solution)/shard_map/slice | solution.py:399
  44.4 0.6 %copy.10 = f32[8,512]{1,0:T(8,128)} copy(f32[8,512]{1,0:T(8,128)S(1)} %get-tuple-element.18) | data formatting | bytes 32768

commit v4 on v3

--- a/solution.py
+++ b/solution.py
@@ -14,6 +14,8 @@
 NEG = -1e30
 NX, NZ, NY, NC = 4, 4, 4, 2
 GROUPS = 4
+PLAN = ((0, 0), (0, 1), (0, 2), (0, 3), (0, 4), (0, 5), (0, 6), (0, 7),
+        (1, 0), (1, 1), (1, 2), (1, 3), (1, 4), (1, 5), (1, 6), (1, 7))
 GW = 256
 NT = (((1,), (1,)), ((), ()))
 NN = (((1,), (0,)), ((), ()))
@@ -210,7 +212,7 @@
     g_far, g_up, g_dn, g_own = order
     steps = [(0, g_far, 0), (0, g_far, 1), (1, g_up, 0), (2, g_dn, 0),
              (1, g_up, 1), (2, g_dn, 1), (3, g_own, 0), (3, g_own, 1)]
-    x_after = {1: [0], 2: [1], 5: [2, 3], 6: [4], 7: [5]}
+    x_after = {1: [0], 2: [1], 6: [2, 3], 7: [4, 5]}
 
     def near_step(i):
         place, g, p = steps[i]
@@ -237,15 +239,16 @@
                 d_st[g, p, b] = stacked(
                     d[b * HALF:(b + 1) * HALF, p * HALF:(p + 1) * HALF]).astype(BF)
 
-    for i in range(len(steps)):
+    def near_all(i):
         near_step(i)
         if i == 1:
             load_og.wait()
             load_w.wait()
         if i % 2:
             dattn_of(i // 2)
-    for i in range(len(steps)):
-        away_step(i)
+
+    for kind, i in PLAN:
+        (near_all, away_step)[kind](i)
 
     def backward(g, p, side):
         dev, b = sides[side]

time: 45.1 us -> 45.1 us (level)
  no operation moved by 1% of the time
where the time goes in v4:
time: 45.1 us; the launch traced here: 44.7 us
  Pallas kernels  42.3 us (94%)
  local copies, waits for them, and re-layouts  1.78 us (4%)
  between operations  0.64 us (1%)
    pallas_call x1, Pallas kernels, on_device(): pl.pallas_call(functools.partial(kernel, n_seq, n_dp), out_shape=outs, in...  42.3 us
    slice x1, local copies, waits for them, and re-layouts, on_device(): return (qkv[0:1], qkv[1:2], qkv[2:3], wg)  1.17 us

profile of v4, /device:TPU:96, one launch (start us, length us, event | category | flops | bytes accessed | tf_op | source)
XLA Modules:
  0.0 44.7 jit_solution(8102472637045630505)
XLA Ops:
  0.6 42.3 %shard_map.84 = (bf16[3,256,1024]{2,1,0:T(8,128)(2,1)S(1)}, f32[8,512]{1,0:T(8,128)S(1)}) custom-call(bf16[256,1024]{1,0:T(8,128)(2,1)} %bitcast.4, bf16[256,1024]{1,0:T(8,128)(2,1)} %bitcast.5, bf16[256,1024]{1,0:T(8,128)(2,1)} %bitcast.6, bf16[256,1024]{1,0:T(8,128)(2,1)} %bitcast.7, bf16[1024,1024]{1,0:T(8,128)(2,1)} %w_h.1), custom_call_target="tpu_custom_call" | custom-call | tf_op jit(solution)/shard_map/pallas_call | solution.py:392
  42.9 1.2 %fusion = (bf16[1,256,1024]{2,1,0:T(8,128)(2,1)}, bf16[1,256,1024]{2,1,0:T(8,128)(2,1)}, bf16[1,256,1024]{2,1,0:T(8,128)(2,1)}) fusion(bf16[3,256,1024]{2,1,0:T(8,128)(2,1)S(1)} %get-tuple-element.6), kind=kLoop, calls=%fused_computation | loop fusion | bytes 3145728 | tf_op jit(solution)/shard_map/slice | solution.py:402
  44.1 0.6 %copy.10 = f32[8,512]{1,0:T(8,128)} copy(f32[8,512]{1,0:T(8,128)S(1)} %get-tuple-element.18) | data formatting | bytes 32768

commit v5 on v4

--- a/solution.py
+++ b/solution.py
@@ -348,8 +348,10 @@
             z_stage(0)
         elif j == 6:
             z_stage(1)
+    for j in range(GROUPS):
+        finish(j)
     y_stage()
-    for j in range(2 * GROUPS):
+    for j in range(GROUPS, 2 * GROUPS):
         finish(j)
     y_finish()
 

time: 45.1 us -> 45.1 us (level)
  no operation moved by 1% of the time
where the time goes in v5:
time: 45.1 us; the launch traced here: 44.7 us
  Pallas kernels  42.3 us (94%)
  local copies, waits for them, and re-layouts  1.78 us (4%)
  between operations  0.64 us (1%)
    pallas_call x1, Pallas kernels, on_device(): pl.pallas_call(functools.partial(kernel, n_seq, n_dp), out_shape=outs, in...  42.3 us
    slice x1, local copies, waits for them, and re-layouts, on_device(): return (qkv[0:1], qkv[1:2], qkv[2:3], wg)  1.17 us

profile of v5, /device:TPU:96, one launch (start us, length us, event | category | flops | bytes accessed | tf_op | source)
XLA Modules:
  0.0 44.7 jit_solution(16566687157413745687)
XLA Ops:
  0.6 42.3 %shard_map.84 = (bf16[3,256,1024]{2,1,0:T(8,128)(2,1)S(1)}, f32[8,512]{1,0:T(8,128)S(1)}) custom-call(bf16[256,1024]{1,0:T(8,128)(2,1)} %bitcast.4, bf16[256,1024]{1,0:T(8,128)(2,1)} %bitcast.5, bf16[256,1024]{1,0:T(8,128)(2,1)} %bitcast.6, bf16[256,1024]{1,0:T(8,128)(2,1)} %bitcast.7, bf16[1024,1024]{1,0:T(8,128)(2,1)} %w_h.1), custom_call_target="tpu_custom_call" | custom-call | tf_op jit(solution)/shard_map/pallas_call | solution.py:394
  42.9 1.2 %fusion = (bf16[1,256,1024]{2,1,0:T(8,128)(2,1)}, bf16[1,256,1024]{2,1,0:T(8,128)(2,1)}, bf16[1,256,1024]{2,1,0:T(8,128)(2,1)}) fusion(bf16[3,256,1024]{2,1,0:T(8,128)(2,1)S(1)} %get-tuple-element.6), kind=kLoop, calls=%fused_computation | loop fusion | bytes 3145728 | tf_op jit(solution)/shard_map/slice | solution.py:404
  44.1 0.6 %copy.10 = f32[8,512]{1,0:T(8,128)} copy(f32[8,512]{1,0:T(8,128)S(1)} %get-tuple-element.18) | data formatting | bytes 32768

commit v6 on v4

--- a/solution.py
+++ b/solution.py
@@ -107,6 +107,8 @@
     for i in range(GROUPS):
         for a in range(2):
             halo(a, 1, away_order[i]).start()
+    for i in range(GROUPS):
+        for a in range(2):
             halo(a, 0, order[i]).start()
 
     row_j = lax.broadcasted_iota(jnp.int32, (HALF, 2 * HALF), 0)

time: 45.1 us -> 45.1 us (level)
  no operation moved by 1% of the time
where the time goes in v6:
time: 45.1 us; the launch traced here: 44.8 us
  Pallas kernels  42.3 us (94%)
  local copies, waits for them, and re-layouts  1.78 us (4%)
  between operations  0.64 us (1%)
    pallas_call x1, Pallas kernels, on_device(): pl.pallas_call(functools.partial(kernel, n_seq, n_dp), out_shape=outs, in...  42.3 us
    slice x1, local copies, waits for them, and re-layouts, on_device(): return (qkv[0:1], qkv[1:2], qkv[2:3], wg)  1.17 us

profile of v6, /device:TPU:96, one launch (start us, length us, event | category | flops | bytes accessed | tf_op | source)
XLA Modules:
  0.0 44.8 jit_solution(16599989907296302432)
XLA Ops:
  0.6 42.3 %shard_map.84 = (bf16[3,256,1024]{2,1,0:T(8,128)(2,1)S(1)}, f32[8,512]{1,0:T(8,128)S(1)}) custom-call(bf16[256,1024]{1,0:T(8,128)(2,1)} %bitcast.4, bf16[256,1024]{1,0:T(8,128)(2,1)} %bitcast.5, bf16[256,1024]{1,0:T(8,128)(2,1)} %bitcast.6, bf16[256,1024]{1,0:T(8,128)(2,1)} %bitcast.7, bf16[1024,1024]{1,0:T(8,128)(2,1)} %w_h.1), custom_call_target="tpu_custom_call" | custom-call | tf_op jit(solution)/shard_map/pallas_call | solution.py:394
  43.0 1.2 %fusion = (bf16[1,256,1024]{2,1,0:T(8,128)(2,1)}, bf16[1,256,1024]{2,1,0:T(8,128)(2,1)}, bf16[1,256,1024]{2,1,0:T(8,128)(2,1)}) fusion(bf16[3,256,1024]{2,1,0:T(8,128)(2,1)S(1)} %get-tuple-element.6), kind=kLoop, calls=%fused_computation | loop fusion | bytes 3145728 | tf_op jit(solution)/shard_map/slice | solution.py:404
  44.2 0.6 %copy.10 = f32[8,512]{1,0:T(8,128)} copy(f32[8,512]{1,0:T(8,128)S(1)} %get-tuple-element.18) | data formatting | bytes 32768
